TPU v7x, 32 devices: a whole 2x2x4 slice. The times are simulated.
32 devices in a mesh: tm: 16 (over z, y, x), space: 2 (over core).
Axes of the slice: x: 2, y: 2, z: 4, core: 2. Of those that a mesh axis runs over, the one named last changes fastest.
Arguments:
- snapshots: float32 [4096, 3, 1024], P('tm', None, 'space'), may hold values from -108 to 108
- weights: float32 [1024], P('space'), may hold values from 0.1 to 1
- start: float32 [2, 15, 8], replicated, may hold values from -6 to 6
Outputs:
- mode_out: float32 [64, 8, 2, 3, 1024], P('tm', None, None, None, 'space')
- energy: float32 [64, 8], P('tm')
All inputs are finite; a program needn't handle non-finite values.
Results may differ from a plain program's by a relative error of at most 0.0003.
Values sent between devices are 32-bit elements; how exact they have to be, the bound alone decides.
A program may use at most 64 MiB of HBM per device.

v0:
```python
import math

import jax
import jax.numpy as jnp
from jax import lax
from jax.sharding import PartitionSpec as P

NF = 64
ITERS = 8


precise = lax.Precision.HIGHEST
epsilon = 1e-06


def shifted(block, axis, distance):
    devices = range(lax.axis_size(axis))
    route = [(i - distance, i) for i in devices if i - distance in devices]
    return lax.ppermute(block, axis, route)


def dft_table(freqs, seg_len):
    length = 2 * seg_len
    times = jnp.arange(length, dtype=jnp.int32)
    freq_ids = jnp.arange(freqs, dtype=jnp.int32)
    turns = jnp.mod(freq_ids[:, None] * times[None, :], length).astype(jnp.float32)
    phase = 2.0 * math.pi / length * turns
    window = 0.5 - 0.5 * jnp.cos(2.0 * math.pi / length * times.astype(jnp.float32))
    factor = 1.0 / jnp.sqrt(jnp.sum(window * window))
    return jnp.concatenate([window * jnp.cos(phase) * factor, -window * jnp.sin(phase) * factor], 0)


def gram_parts(spectra, col_weights, total_points):
    weighted = spectra * col_weights
    grams = jnp.einsum("nrfc,msfc->frnsm", spectra, weighted, precision=precise)
    gram_re = (grams[:, 0, :, 0, :] + grams[:, 1, :, 1, :]) / total_points
    gram_im = (grams[:, 0, :, 1, :] - grams[:, 1, :, 0, :]) / total_points
    return (gram_re, gram_im)


def apply_gram(gram_re, gram_im, vec_re, vec_im):
    img_re = jnp.einsum("fnm,fmk->fnk", gram_re, vec_re, precision=precise) - jnp.einsum(
        "fnm,fmk->fnk", gram_im, vec_im, precision=precise
    )
    img_im = jnp.einsum("fnm,fmk->fnk", gram_re, vec_im, precision=precise) + jnp.einsum(
        "fnm,fmk->fnk", gram_im, vec_re, precision=precise
    )
    return (img_re, img_im)


def orthonormal(img_re, img_im):
    cols_re = []
    cols_im = []
    for column in range(img_re.shape[-1]):
        part_re = img_re[..., column]
        part_im = img_im[..., column]
        if column > 0:
            prev_re = jnp.stack(cols_re, -1)
            prev_im = jnp.stack(cols_im, -1)
            for repeat in range(2):
                coef_re = jnp.sum(
                    prev_re * part_re[..., None] + prev_im * part_im[..., None], axis=1
                )
                coef_im = jnp.sum(
                    prev_re * part_im[..., None] - prev_im * part_re[..., None], axis=1
                )
                part_re = part_re - jnp.sum(
                    prev_re * coef_re[:, None, :] - prev_im * coef_im[:, None, :], axis=-1
                )
                part_im = part_im - jnp.sum(
                    prev_re * coef_im[:, None, :] + prev_im * coef_re[:, None, :], axis=-1
                )
        inverse = 1.0 / jnp.sqrt(jnp.sum(part_re * part_re + part_im * part_im, axis=1) + epsilon)
        cols_re.append(part_re * inverse[:, None])
        cols_im.append(part_im * inverse[:, None])
    return (jnp.stack(cols_re, -1), jnp.stack(cols_im, -1))


def subspace(gram_re, gram_im, start):
    shape = (gram_re.shape[0], start.shape[1], start.shape[2])
    vec_re = jnp.broadcast_to(start[0], shape)
    vec_im = jnp.broadcast_to(start[1], shape)
    for sweep in range(ITERS):
        img_re, img_im = apply_gram(gram_re, gram_im, vec_re, vec_im)
        vec_re, vec_im = orthonormal(img_re, img_im)
    return (vec_re, vec_im)


def project(spectra, vec_re, vec_im):
    real_rows = spectra[:, 0]
    imag_rows = spectra[:, 1]
    mode_re = jnp.einsum("nfc,fnk->fkc", real_rows, vec_re, precision=precise) - jnp.einsum(
        "nfc,fnk->fkc", imag_rows, vec_im, precision=precise
    )
    mode_im = jnp.einsum("nfc,fnk->fkc", real_rows, vec_im, precision=precise) + jnp.einsum(
        "nfc,fnk->fkc", imag_rows, vec_re, precision=precise
    )
    return (mode_re, mode_im)


def body(snapshots, weights, start):
    seg_len, components, points = snapshots.shape
    columns = components * points
    samples = snapshots.reshape(seg_len, columns)
    basis = dft_table(NF, seg_len)
    tm_count = lax.axis_size("tm")
    blocks = tm_count - 1
    later = shifted(samples, "tm", -1)
    window_rows = jnp.concatenate([samples, later], 0)
    spectrum = jnp.dot(basis, window_rows, precision=precise)
    arrived = lax.all_to_all(
        spectrum.reshape(1, 2, NF, columns), "tm", split_axis=2, concat_axis=0, tiled=True
    )
    spectra = arrived[:blocks]
    col_weights = jnp.tile(weights, components)
    total_points = points * lax.axis_size("space")
    gram_re, gram_im = gram_parts(spectra, col_weights, total_points)
    gram_re, gram_im = lax.psum((gram_re, gram_im), "space")
    vec_re, vec_im = subspace(gram_re, gram_im, start)
    mode_re, mode_im = project(spectra, vec_re, vec_im)
    partial_energy = (
        jnp.sum((mode_re * mode_re + mode_im * mode_im) * col_weights, axis=-1) / total_points
    )
    energy = lax.psum(partial_energy, "space")
    inverse = 1.0 / jnp.sqrt(energy + epsilon)
    mode_out = jnp.stack([mode_re, mode_im], 2) * inverse[:, :, None, None]
    freq_count = mode_out.shape[0]
    return (mode_out.reshape(freq_count, mode_out.shape[1], 2, components, points), energy)


def solution(mesh):
    in_specs = (P("tm", None, "space"), P("space"), P())
    out_specs = (P("tm", None, None, None, "space"), P("tm", None))
    return jax.shard_map(body, mesh=mesh, in_specs=in_specs, out_specs=out_specs, check_vma=False)
```

profile of v0, /device:TPU:17, one launch (start us, length us, event | category | flops | bytes accessed | tf_op | source)
XLA Modules:
  0.0 130.2 jit_solution(17040012056975748923)
XLA Ops:
  0.6 1.9 %copy.460 = f32[256,3,512]{0,2,1:T(8,128)S(1)} copy(f32[256,3,512]{2,0,1:T(8,128)} %param.3) | data formatting | bytes 3145728 | tf_op args[0]
  2.5 4.0 %collective-permute-start = (f32[256,1536]{0,1:T(8,128)S(1)}, f32[256,1536]{0,1:T(8,128)S(1)}, u32[]{:S(2)}, u32[]{:S(2)}) collective-permute-start(f32[256,1536]{0,1:T(8,128)S(1)} %bitcast.877), channel_id=1, source_target_pairs={{2,0},{4,2},{6,4},{8,6},{10,8},{12,10},{14,12},{16,14},{18,16},{20... | collective-permute-start | bytes 4718600 | tf_op jit(solution)/shard_map/ppermute | solution.py:19
  6.5 0.6 multiply_reduce_fusion.1
  7.9 0.5 multiply_multiply_fusion
  8.5 31.2 %collective-permute-done = f32[256,1536]{0,1:T(8,128)S(1)} collective-permute-done((f32[256,1536]{0,1:T(8,128)S(1)}, f32[256,1536]{0,1:T(8,128)S(1)}, u32[]{:S(2)}, u32[]{:S(2)}) %collective-permute-start) | collective-permute-done | bytes 1572896 | tf_op jit(solution)/shard_map/ppermute | solution.py:19
  39.7 3.3 %fusion = f32[128,1536]{1,0:T(8,128)S(1)} fusion(f32[256,1536]{0,1:T(8,128)S(1)} %collective-permute-done, f32[256,1536]{0,1:T(8,128)S(1)} %bitcast.878, f32[64,512]{1,0:T(8,128)S(1)} %get-tuple-element.722, f32[64,512]{1,0:T(8,128)S(1)} %get-tuple-element.723), kind=kOutput, calls=%fused_computation | convolution fusion | flops 1208811520 | bytes 4194304 | tf_op jit(solution)/shard_map/dot_general | solution.py:110
  43.0 1.5 %copy.461 = f32[1,2,64,1536]{3,1,0,2:T(2,128)} copy(f32[1,2,64,1536]{3,2,1,0:T(8,128)S(1)} %bitcast.879) | data formatting | bytes 1572864 | tf_op jit(solution)/shard_map/reshape | solution.py:112
  44.5 7.3 %all-to-all-start = ((f32[1,2,64,1536]{3,1,0,2:T(2,128)}), f32[1,2,64,1536]{3,1,0,2:T(2,128)S(1)}, u32[]{:S(2)}, u32[]{:S(2)}) async-start(f32[1,2,64,1536]{3,1,0,2:T(2,128)} %copy.461), calls=%async_computation | async-start | bytes 1572864 | tf_op jit(solution)/shard_map/all_to_all | solution.py:111
  51.9 18.5 %all-to-all-done = f32[1,2,64,1536]{3,1,0,2:T(2,128)S(1)} async-done(((f32[1,2,64,1536]{3,1,0,2:T(2,128)}), f32[1,2,64,1536]{3,1,0,2:T(2,128)S(1)}, u32[]{:S(2)}, u32[]{:S(2)}) %all-to-all-start) | async-done | bytes 786464 | tf_op jit(solution)/shard_map/all_to_all | solution.py:111
  70.4 0.5 copy.724
  70.9 3.4 %convolution_bitcast_fusion = f32[4,2,15,2,15]{2,4,1,3,0:T(8,128)S(1)} fusion(f32[16,1,2,4,1536]{4,0,2,3,1:T(8,128)S(1)} %bitcast.876, f32[1536]{0:T(1024)S(1)} %mul.8264), kind=kOutput, calls=%fused_computation.6 | convolution fusion | flops 66539520 | bytes 1595456 | tf_op jit(solution)/shard_map/nrfc,msfc->frnsm/dot_general | solution.py:35
  74.3 5.0 %all-reduce = (f32[4,15,15]{1,2,0:T(8,128)S(1)}, f32[4,15,15]{1,2,0:T(8,128)S(1)}) all-reduce(f32[4,15,15]{1,2,0:T(8,128)S(1)} %get-tuple-element.477, f32[4,15,15]{1,2,0:T(8,128)S(1)} %get-tuple-element.476), channel_id=1, replica_groups=mesh['tm'=16,'space'=2] {'space'}, use_global_device_ids=true, to_apply=%region_1.2 | all-reduce | flops 1800 | bytes 14400 | tf_op jit(solution)/shard_map/psum | solution.py:118
  79.3 0.2 fusion.28
  79.4 0.2 fusion.24
  79.6 0.2 convolution_subtract_fusion.8
  79.8 0.2 convolution_add_fusion.8
  80.1 0.2 add_reduce_fusion.270
  80.3 0.2 add_reduce_fusion.269
  80.5 0.2 add_reduce_fusion.268
  84.9 0.2 fusion.64
  85.3 0.2 convolution_subtract_fusion.7
  85.4 0.2 convolution_add_fusion.7
  85.7 0.2 add_reduce_fusion.260
  85.9 0.2 add_reduce_fusion.259
  86.1 0.2 add_reduce_fusion.258
  90.9 0.2 convolution_subtract_fusion.6
  91.1 0.2 convolution_add_fusion.6
  91.4 0.2 add_reduce_fusion.250
  91.6 0.2 add_reduce_fusion.249
  91.8 0.2 add_reduce_fusion.248
  96.4 0.2 fusion.69
  96.6 0.2 convolution_subtract_fusion.5
  96.8 0.2 convolution_add_fusion.5
  97.1 0.2 add_reduce_fusion.240
  97.2 0.2 add_reduce_fusion.239
  97.4 0.2 add_reduce_fusion.238
  102.2 0.2 convolution_subtract_fusion.4
  102.4 0.2 convolution_add_fusion.4
  102.7 0.2 add_reduce_fusion.230
  102.9 0.2 add_reduce_fusion.229
  103.1 0.2 add_reduce_fusion.228
  107.9 0.2 convolution_subtract_fusion.3
  108.1 0.2 convolution_add_fusion.3
  108.4 0.2 add_reduce_fusion.220
  108.6 0.2 add_reduce_fusion.219
  108.8 0.2 add_reduce_fusion.218
  113.8 0.2 convolution_subtract_fusion.2
  114.0 0.2 convolution_add_fusion.2
  114.3 0.2 add_reduce_fusion.210
  114.4 0.2 add_reduce_fusion.209
  114.6 0.2 add_reduce_fusion.208
  119.4 0.2 convolution_subtract_fusion.1
  119.6 0.2 convolution_add_fusion.1
  119.9 0.2 add_reduce_fusion.200
  120.1 0.2 add_reduce_fusion.199
  120.3 0.2 add_reduce_fusion.198
  124.8 0.3 fusion.9
  125.1 0.3 fusion.10
  125.4 0.3 convolution_subtract_fusion
  125.8 0.4 multiply_reduce_fusion
  126.2 0.2 copy.688
  126.4 2.5 %psum.23 = f32[4,8]{1,0:T(4,128)S(1)} all-reduce(f32[4,8]{1,0:T(4,128)S(1)} %broadcast_multiply_fusion), channel_id=1, replica_groups=mesh['tm'=16,'space'=2] {'space'}, use_global_device_ids=true, to_apply=%region_484.485 | all-reduce | flops 32 | bytes 256 | tf_op jit(solution)/shard_map/psum | solution.py:124
  128.9 0.2 copy.687
  129.1 1.1 maximum_multiply_fusion
  (555 shorter events, 36.0 us)
Async XLA Ops:
  2.5 37.2 %collective-permute-start = (f32[256,1536]{0,1:T(8,128)S(1)}, f32[256,1536]{0,1:T(8,128)S(1)}, u32[]{:S(2)}, u32[]{:S(2)}) collective-permute-start(f32[256,1536]{0,1:T(8,128)S(1)} %bitcast.877), channel_id=1, source_target_pairs={{2,0},{4,2},{6,4},{8,6},{10,8},{12,10},{14,12},{16,14},{18,16},{20... | collective-permute-start | bytes 4718600 | tf_op jit(solution)/shard_map/ppermute | solution.py:19
  43.0 8.9 %copy-start.2 = (f32[512]{0:T(512)S(1)}, f32[512]{0:T(512)}, u32[]{:S(2)}) copy-start(f32[512]{0:T(512)} %param.4) | copy-start | bytes 6148
  43.0 8.9 %copy-start = (f32[2,15,8]{1,2,0:T(8,128)S(1)}, f32[2,15,8]{1,2,0:T(8,128)}, u32[]{:S(2)}) copy-start(f32[2,15,8]{1,2,0:T(8,128)} %param.5) | copy-start | bytes 2884
  44.5 25.9 %all-to-all-start = ((f32[1,2,64,1536]{3,1,0,2:T(2,128)}), f32[1,2,64,1536]{3,1,0,2:T(2,128)S(1)}, u32[]{:S(2)}, u32[]{:S(2)}) async-start(f32[1,2,64,1536]{3,1,0,2:T(2,128)} %copy.461), calls=%async_computation | async-start | bytes 1572864 | tf_op jit(solution)/shard_map/all_to_all | solution.py:111
  128.9 1.3 %copy-start.1 = (f32[4,8]{1,0:T(4,128)}, f32[4,8]{1,0:T(4,128)S(1)}, u32[]{:S(2)}) copy-start(f32[4,8]{1,0:T(4,128)S(1)} %psum.23) | copy-start | bytes 388
where the time goes:
time: 132 us; the launch traced here: 130 us
  waiting for transfers between devices  49.7 us (38%)
  other arithmetic  38.5 us (29%)
  matrix products  13.4 us (10%)
  starting transfers between devices  11.3 us (9%)
  blocking collectives  7.46 us (6%)
  local copies, waits for them, and re-layouts  6.57 us (5%)
  between operations  3.27 us (2%)
    ppermute x1, waiting for transfers between devices, shifted(): return lax.ppermute(block, axis, route)  31.2 us
    all_to_all x1, waiting for transfers between devices, body(): lax.all_to_all(spectrum.reshape(1, 2, NF, columns), 'tm', split_axis=2, c...  18.5 us
    reduce_sum x112, other arithmetic, orthonormal(): jnp.sum(prev_re * part_re[..., None] + prev_im * part_im[..., None], axis=1)  13 us
    reduce_sum x96, other arithmetic, orthonormal(): jnp.sum(prev_re * coef_re[:, None, :] - prev_im * coef_im[:, None, :], ax...  9.33 us
    reduce_sum x64, other arithmetic, orthonormal(): jnp.sum(part_re * part_re + part_im * part_im, axis=1) + epsilon  8.27 us
    all_to_all x1, starting transfers between devices, body(): lax.all_to_all(spectrum.reshape(1, 2, NF, columns), 'tm', split_axis=2, c...  7.34 us
    psum x1, blocking collectives, body(): gram_re, gram_im = lax.psum((gram_re, gram_im), 'space')  4.99 us
    mul x56, other arithmetic, orthonormal(): cols_re.append(part_re * inverse[:, None])  4.27 us
  transfers between devices with their start and end apart: 2, of which 2 were waited for; matrix products, arithmetic and copies ran while one was open for 1% of the time, Pallas kernels for 0%

commit v1 on v0

v1 whole, which is shorter than its diff:
```python
import functools
import math

import numpy as np
import jax
import jax.numpy as jnp
from jax import lax
from jax.experimental import pallas as pl
from jax.experimental.pallas import tpu as pltpu
from jax.sharding import PartitionSpec as P

NF = 64
ITERS = 8

precise = lax.Precision.HIGHEST
epsilon = 1e-06


def segment_table(owners, seg_len):
    length = 2 * seg_len
    per = NF // owners
    t = np.arange(length)
    hann = 0.5 - 0.5 * np.cos(2.0 * np.pi / length * t)
    factor = 1.0 / np.sqrt(np.sum(hann * hann))
    freqs = np.arange(owners)[:, None] * per + np.arange(-1, per + 1)[None, :]
    turns = np.mod(freqs[:, :, None] * np.arange(seg_len), length)
    phase = 2.0 * np.pi / length * turns
    table = np.stack([np.cos(phase), -np.sin(phase)], 1) * factor
    return table.astype(np.float32)


def subspace_kernel(modes, mr_ref, mi_ref, start_ref, vec_ref, energy_ref):
    n = mr_ref.shape[0]

    def apply(vec):
        out = []
        for k in range(modes):
            vr, vi = vec[k]
            wr = wi = None
            for j in range(n):
                br, bi = vr[j : j + 1], vi[j : j + 1]
                ar, ai = mr_ref[j], mi_ref[j]
                pr, pi = ar * br - ai * bi, ar * bi + ai * br
                wr = pr if wr is None else wr + pr
                wi = pi if wi is None else wi + pi
            out.append((wr, wi))
        return out

    def total(x):
        return jnp.sum(x, axis=0, keepdims=True)

    def coefs(u, w):
        return total(u[0] * w[0] + u[1] * w[1]), total(u[0] * w[1] - u[1] * w[0])

    def less(w, u, c):
        return w[0] - (u[0] * c[0] - u[1] * c[1]), w[1] - (u[0] * c[1] + u[1] * c[0])

    def sweep(_, flat):
        vec = [(flat[2 * k], flat[2 * k + 1]) for k in range(modes)]
        images = apply(vec)
        rest = list(images)
        done = []
        for k in range(modes):
            w = rest[k]
            if done:
                cs = [coefs(u, w) for u in done]
                for u, c in zip(done, cs):
                    w = less(w, u, c)
            inverse = 1.0 / jnp.sqrt(total(w[0] * w[0] + w[1] * w[1]) + epsilon)
            u = (w[0] * inverse, w[1] * inverse)
            done.append(u)
            for later in range(k + 1, modes):
                rest[later] = less(rest[later], u, coefs(u, images[later]))
        return tuple(x for u in done for x in u)

    shape = mr_ref.shape[1:]
    flat = tuple(
        jnp.broadcast_to(start_ref[c, k], shape) for k in range(modes) for c in range(2)
    )
    flat = lax.fori_loop(0, ITERS, sweep, flat)
    vec = [(flat[2 * k], flat[2 * k + 1]) for k in range(modes)]
    images = apply(vec)
    for k in range(modes):
        (vr, vi), (wr, wi) = vec[k], images[k]
        energy = total(vr * wr + vi * wi)
        inverse = 1.0 / jnp.sqrt(energy + epsilon)
        energy_ref[k : k + 1] = energy
        vec_ref[0, k] = vr * inverse
        vec_ref[1, k] = vi * inverse


def subspace(gram_re, gram_im, start):
    freqs, n, _ = gram_re.shape
    modes = start.shape[2]
    start = jnp.pad(start, ((0, 0), (0, n - start.shape[1]), (0, 0)))
    start = start.transpose(0, 2, 1)[..., None]
    spec = pl.BlockSpec(memory_space=pltpu.VMEM)
    return pl.pallas_call(
        functools.partial(subspace_kernel, modes),
        out_shape=(
            jax.ShapeDtypeStruct((2, modes, n, freqs), jnp.float32),
            jax.ShapeDtypeStruct((modes, freqs), jnp.float32),
        ),
        in_specs=[spec] * 3,
        out_specs=(spec, spec),
    )(gram_re.transpose(2, 1, 0), gram_im.transpose(2, 1, 0), start)


def body(snapshots, weights, start):
    seg_len, components, points = snapshots.shape
    columns = components * points
    samples = snapshots.reshape(seg_len, columns)
    owners = lax.axis_size("tm")
    freqs = NF // owners
    table = segment_table(owners, seg_len)
    segment = jnp.dot(table.reshape(-1, seg_len), samples, precision=precise)
    arrived = lax.all_to_all(
        segment.reshape(owners, 2, freqs + 2, columns), "tm", split_axis=0, concat_axis=0, tiled=True
    )
    first = lax.axis_index("tm") * freqs - 1
    signs = 1.0 - 2.0 * jnp.mod(first + owners * freqs * 2 + jnp.arange(freqs + 2), 2).astype(jnp.float32)
    pairs = arrived[:-1] + signs[:, None] * arrived[1:]
    spectra = 0.5 * pairs[:, :, 1:-1] - 0.25 * (pairs[:, :, :-2] + pairs[:, :, 2:])
    blocks = owners - 1
    padded = (blocks + 7) // 8 * 8
    spectra = jnp.pad(spectra, ((0, padded - blocks), (0, 0), (0, 0), (0, 0)))
    col_weights = jnp.tile(weights, components)
    total_points = points * lax.axis_size("space")
    weighted = spectra * col_weights
    grams = jnp.einsum("nrfc,msfc->frnsm", spectra, weighted, precision=precise)
    gram_re = (grams[:, 0, :, 0, :] + grams[:, 1, :, 1, :]) / total_points
    gram_im = (grams[:, 0, :, 1, :] - grams[:, 1, :, 0, :]) / total_points
    gram_re, gram_im = lax.psum((gram_re, gram_im), "space")
    vec, energy = subspace(gram_re, gram_im, start)
    vr, vi = vec[0], vec[1]
    mix = jnp.stack([jnp.stack([vr, -vi], 0), jnp.stack([vi, vr], 0)], 0)
    modes = jnp.einsum("nrfc,srknf->fksc", spectra, mix, precision=precise)
    return modes.reshape(freqs, modes.shape[1], 2, components, points), energy.T


def solution(mesh):
    in_specs = (P("tm", None, "space"), P("space"), P())
    out_specs = (P("tm", None, None, None, "space"), P("tm", None))
    return jax.shard_map(body, mesh=mesh, in_specs=in_specs, out_specs=out_specs, check_vma=False)
```

time: 132 us -> 64.3 us (0.49)
  the two profiles are of different devices: /device:TPU:17 before, /device:TPU:9 now
where the time goes in v1:
time: 64.3 us; the launch traced here: 63.9 us
  waiting for transfers between devices  26.3 us (41%)
  local copies, waits for them, and re-layouts  7.82 us (12%)
  Pallas kernels  7.79 us (12%)
  blocking collectives  6.97 us (11%)
  starting transfers between devices  6.79 us (11%)
  matrix products  5.65 us (9%)
  other arithmetic  1.79 us (3%)
  between operations  0.74 us (1%)
    all_to_all x1, waiting for transfers between devices, body(): lax.all_to_all(segment.reshape(owners, 2, freqs + 2, columns), 'tm', spli...  26.3 us
    pallas_call x1, Pallas kernels, subspace(): pl.pallas_call(functools.partial(subspace_kernel, modes), out_shape=(jax....  7.79 us
    psum x1, blocking collectives, body(): gram_re, gram_im = lax.psum((gram_re, gram_im), 'space')  6.97 us
    all_to_all x1, starting transfers between devices, body(): lax.all_to_all(segment.reshape(owners, 2, freqs + 2, columns), 'tm', spli...  6.79 us
    unnamed x11, local copies, waits for them, and re-layouts  3.63 us
    dot_general x1, matrix products, body(): grams = jnp.einsum('nrfc,msfc->frnsm', spectra, weighted, precision=precise)  3.37 us
    dot_general x1, local copies, waits for them, and re-layouts, body(): segment = jnp.dot(table.reshape(-1, seg_len), samples, precision=precise)  1.94 us
    dot_general x1, matrix products, body(): segment = jnp.dot(table.reshape(-1, seg_len), samples, precision=precise)  1.76 us
  transfers between devices with their start and end apart: 1, of which 1 were waited for; matrix products, arithmetic and copies ran while one was open for 1% of the time, Pallas kernels for 0%

profile of v1, /device:TPU:9, one launch (start us, length us, event | category | flops | bytes accessed | tf_op | source)
XLA Modules:
  0.0 63.9 jit_solution(10569029474671351492)
XLA Ops:
  0.6 0.0 copy-start
  0.6 1.9 %copy.51 = f32[256,3,512]{0,2,1:T(8,128)S(1)} copy(f32[256,3,512]{2,0,1:T(8,128)} %param.4) | data formatting | bytes 3145728 | tf_op args[0]
  2.6 0.0 copy-done
  2.6 1.8 %fusion.24 = f32[16,2,6,1536]{3,0,2,1:T(8,128)S(1)} fusion(f32[16,2,6,256]{3,0,2,1:T(8,128)S(1)} %copy-done, f32[256,1536,1,1]{0,1,3,2:T(8,128)S(1)} %bitcast.41), kind=kOutput, calls=%fused_computation.37 | convolution fusion | flops 905969664 | bytes 2949120 | tf_op jit(solution)/shard_map/dot_general | solution.py:116
  4.3 1.9 %copy.53 = f32[16,2,6,1536]{3,1,2,0:T(2,128)} copy(f32[16,2,6,1536]{3,0,2,1:T(8,128)S(1)} %fusion.24) | data formatting | bytes 2359296 | tf_op jit(solution)/shard_map/dot_general | solution.py:116
  6.3 0.0 copy-start.3
  6.3 0.0 copy-start.1
  6.3 6.8 %all-to-all-start = ((f32[16,2,6,1536]{3,1,2,0:T(2,128)}), f32[16,2,6,1536]{3,1,2,0:T(2,128)S(1)}, u32[]{:S(2)}, u32[]{:S(2)}) async-start(f32[16,2,6,1536]{3,1,2,0:T(2,128)} %copy.53), calls=%async_computation | async-start | bytes 2359296 | tf_op jit(solution)/shard_map/all_to_all | solution.py:117
  13.1 0.0 copy-done.3
  13.1 0.0 copy-done.1
  13.1 0.8 %copy.57.start_ref = f32[2,8,16,1]{3,2,1,0:T(8,128)} copy(f32[2,8,16,1]{2,1,0,3:T(8,128)S(1)} %pad_bitcast_fusion) | data formatting | bytes 2048 | tf_op jit(solution)/shard_map/broadcast_in_dim | solution.py:96
  14.0 26.3 %all-to-all-done = f32[16,2,6,1536]{3,1,2,0:T(2,128)S(1)} async-done(((f32[16,2,6,1536]{3,1,2,0:T(2,128)}), f32[16,2,6,1536]{3,1,2,0:T(2,128)S(1)}, u32[]{:S(2)}, u32[]{:S(2)}) %all-to-all-start) | async-done | bytes 1179680 | tf_op jit(solution)/shard_map/all_to_all | solution.py:117
  40.3 0.6 fusion.23
  40.9 0.7 %fusion = f32[15,2,6,1536]{3,0,1,2:T(8,128)S(1)} fusion(f32[15,2,6,1536]{3,1,2,0:T(2,128)S(1)} %get-tuple-element.19, f32[15,2,6,1536]{3,1,2,0:T(2,128)S(1)} %get-tuple-element.18, f32[6]{0:T(128)S(1)} %fusion.19), kind=kLoop, calls=%fused_computation.1 | loop fusion | flops 552960 | bytes 3317784 | tf_op jit(solution)/shard_map/add | solution.py:122
  41.6 0.1 fusion.2
  41.7 3.4 %fusion.5 = f32[4,16,2,16,2]{3,1,4,2,0:T(8,128)S(1)} fusion(f32[15,2,4,1536]{3,0,1,2:T(8,128)S(1)} %fusion.2, f32[1536]{0:T(1024)S(1)} %mul.48), kind=kOutput, calls=%fused_computation.8 | convolution fusion | flops 75694080 | bytes 759808 | tf_op jit(solution)/shard_map/nrfc,msfc->frnsm/dot_general | solution.py:130
  45.1 0.5 copy.56
  45.6 7.0 %all-reduce.2 = (f32[16,16,4]{2,1,0:T(8,128)}, f32[16,16,4]{2,1,0:T(8,128)}) all-reduce(f32[16,16,4]{2,1,0:T(8,128)S(1)} %get-tuple-element.21, f32[16,16,4]{2,1,0:T(8,128)S(1)} %get-tuple-element.20), channel_id=1, replica_groups=mesh['tm'=16,'space'=2] {'space'}, use_global_device_ids=true, to_apply=%region_0.1 | all-reduce | flops 2048 | bytes 16384 | tf_op jit(solution)/shard_map/psum | solution.py:133
  52.6 7.8 %shard_map.59 = (f32[2,8,16,4]{3,2,1,0:T(8,128)}, f32[8,4]{1,0:T(8,128)}) custom-call(f32[16,16,4]{2,1,0:T(8,128)} %get-tuple-element.16.mr_ref, f32[16,16,4]{2,1,0:T(8,128)} %get-tuple-element.17.mi_ref, f32[2,8,16,1]{3,2,1,0:T(8,128)} %copy.57.start_ref), custom_call_target="tpu_custom_call" | custom-call | tf_op jit(solution)/shard_map/pallas_call | solution.py:98
  60.4 0.9 %slice_negate_fusion = (f32[1,8,16,4]{3,2,1,0:T(8,128)S(1)}, f32[1,8,16,4]{3,2,1,0:T(8,128)S(1)}, f32[1,8,16,4]{3,2,1,0:T(8,128)S(1)}) fusion(f32[2,8,16,4]{3,2,1,0:T(8,128)} %get-tuple-element.4), kind=kLoop, calls=%fused_computation.35 | loop fusion | flops 512 | bytes 10240 | tf_op jit(solution)/shard_map/neg | solution.py:136
  61.3 0.1 copy.58
  61.4 0.0 copy-start.2
  61.4 0.1 copy.59
  61.5 0.1 copy.60
  61.7 0.5 fusion.3
  62.2 1.1 %copy.63 = f32[4,8,2,3,512]{4,2,3,1,0:T(2,128)} copy(f32[4,8,2,3,512]{4,1,3,2,0:T(8,128)S(1)} %bitcast.43) | data formatting | bytes 786432
  63.3 0.0 copy-done.2
  63.3 0.7 %copy.64 = f32[4,8]{1,0:T(4,128)} copy(f32[4,8]{0,1:T(8,128)S(1)} %bitcast.44) | data formatting | bytes 256
  (6 shorter events, 0.1 us)
Async XLA Ops:
  0.6 1.9 %copy-start = (f32[16,2,6,256]{3,0,2,1:T(8,128)S(1)}, f32[16,2,6,256]{3,0,2,1:T(8,128)}, u32[]{:S(2)}) copy-start(f32[16,2,6,256]{3,0,2,1:T(8,128)} %constant.50) | copy-start | bytes 589828
  6.3 6.8 %copy-start.3 = (f32[512]{0:T(512)S(1)}, f32[512]{0:T(512)}, u32[]{:S(2)}) copy-start(f32[512]{0:T(512)} %param.5) | copy-start | bytes 6148
  6.3 6.8 %copy-start.1 = (f32[2,15,8]{1,2,0:T(8,128)S(1)}, f32[2,15,8]{1,2,0:T(8,128)}, u32[]{:S(2)}) copy-start(f32[2,15,8]{1,2,0:T(8,128)} %param.6) | copy-start | bytes 2884
  6.3 34.0 %all-to-all-start = ((f32[16,2,6,1536]{3,1,2,0:T(2,128)}), f32[16,2,6,1536]{3,1,2,0:T(2,128)S(1)}, u32[]{:S(2)}, u32[]{:S(2)}) async-start(f32[16,2,6,1536]{3,1,2,0:T(2,128)} %copy.53), calls=%async_computation | async-start | bytes 2359296 | tf_op jit(solution)/shard_map/all_to_all | solution.py:117
  61.4 1.9 %copy-start.2 = (f32[8,4]{1,0:T(8,128)S(1)}, f32[8,4]{1,0:T(8,128)}, u32[]{:S(2)}) copy-start(f32[8,4]{1,0:T(8,128)} %get-tuple-element.5) | copy-start | bytes 388

commit v2 on v1

--- a/solution.py
+++ b/solution.py
@@ -27,6 +27,100 @@
     phase = 2.0 * np.pi / length * turns
     table = np.stack([np.cos(phase), -np.sin(phase)], 1) * factor
     return table.astype(np.float32)
+
+
+def exchange_kernel(table_ref, samples_ref, out_ref, send_ref, send_sems, recv_sems):
+    owners, rows, half = send_ref.shape
+    count = rows // 2
+    points = samples_ref.shape[2]
+    group = owners // 2
+    me = lax.axis_index("tm")
+    near = me // group
+    far = 1 - near
+
+    barrier = pltpu.get_barrier_semaphore()
+
+    @pl.loop(1, owners)
+    def _(s):
+        other = lax.rem(me + s, owners)
+        pl.semaphore_signal(barrier, inc=1, device_id={"tm": other}, device_id_type=pl.DeviceIdType.MESH)
+
+    def transform(side):
+        for c in range(samples_ref.shape[0]):
+            part = jnp.dot(
+                table_ref[side],
+                samples_ref[c],
+                precision=precise,
+                preferred_element_type=jnp.float32,
+            )
+            low, high = c * points, (c + 1) * points
+            for q in range(2):
+                begin, end = max(low, q * half), min(high, (q + 1) * half)
+                if begin >= end:
+                    continue
+                for i in range(group):
+                    send_ref[
+                        side * group + i, q * count : (q + 1) * count, begin - q * half : end - q * half
+                    ] = part[i * count : (i + 1) * count, begin - low : end - low]
+
+    def copy(source, target):
+        return pltpu.make_async_remote_copy(
+            src_ref=send_ref.at[target],
+            dst_ref=out_ref.at[source],
+            send_sem=send_sems.at[target],
+            recv_sem=recv_sems.at[source],
+            device_id={"tm": target},
+            device_id_type=pl.DeviceIdType.MESH,
+        )
+
+    transform(far)
+    pl.semaphore_wait(barrier, owners - 1)
+
+    @pl.loop(0, group)
+    def _(s):
+        copy(me, far * group + lax.rem(me + s, group)).start()
+
+    transform(near)
+
+    @pl.loop(1, group)
+    def _(s):
+        copy(me, near * group + lax.rem(me + s, group)).start()
+
+    out_ref[me] = send_ref[me]
+
+    @pl.loop(1, owners)
+    def _(s):
+        other = lax.rem(me + s, owners)
+        copy(me, other).wait_send()
+        pltpu.make_async_remote_copy(
+            src_ref=send_ref.at[other],
+            dst_ref=out_ref.at[other],
+            send_sem=send_sems.at[other],
+            recv_sem=recv_sems.at[other],
+            device_id={"tm": other},
+            device_id_type=pl.DeviceIdType.MESH,
+        ).wait_recv()
+
+
+def exchange(table, samples):
+    owners, parts, freqs, seg_len = table.shape
+    half = samples.shape[0] * samples.shape[2] // 2
+    rows = 2 * parts * freqs
+    spec = pl.BlockSpec(memory_space=pltpu.VMEM)
+    return pl.pallas_call(
+        exchange_kernel,
+        out_shape=jax.ShapeDtypeStruct((owners, rows, half), jnp.float32),
+        in_specs=[spec] * 2,
+        out_specs=spec,
+        scratch_shapes=[
+            pltpu.VMEM((owners, rows, half), jnp.float32),
+            pltpu.SemaphoreType.DMA((owners,)),
+            pltpu.SemaphoreType.DMA((owners,)),
+        ],
+        compiler_params=pltpu.CompilerParams(
+            collective_id=0, has_side_effects=True, vmem_limit_bytes=40 * 1024 * 1024
+        ),
+    )(table.reshape(2, -1, seg_len), samples)
 
 
 def subspace_kernel(modes, mr_ref, mi_ref, start_ref, vec_ref, energy_ref):
@@ -109,18 +203,16 @@
 def body(snapshots, weights, start):
     seg_len, components, points = snapshots.shape
     columns = components * points
-    samples = snapshots.reshape(seg_len, columns)
+    samples = snapshots.transpose(1, 0, 2)
     owners = lax.axis_size("tm")
     freqs = NF // owners
     table = segment_table(owners, seg_len)
-    segment = jnp.dot(table.reshape(-1, seg_len), samples, precision=precise)
-    arrived = lax.all_to_all(
-        segment.reshape(owners, 2, freqs + 2, columns), "tm", split_axis=0, concat_axis=0, tiled=True
-    )
+    arrived = exchange(table, samples).reshape(owners, 2, 2, freqs + 2, columns // 2)
     first = lax.axis_index("tm") * freqs - 1
     signs = 1.0 - 2.0 * jnp.mod(first + owners * freqs * 2 + jnp.arange(freqs + 2), 2).astype(jnp.float32)
     pairs = arrived[:-1] + signs[:, None] * arrived[1:]
-    spectra = 0.5 * pairs[:, :, 1:-1] - 0.25 * (pairs[:, :, :-2] + pairs[:, :, 2:])
+    spectra = 0.5 * pairs[..., 1:-1, :] - 0.25 * (pairs[..., :-2, :] + pairs[..., 2:, :])
+    spectra = jnp.concatenate([spectra[:, 0], spectra[:, 1]], -1)
     blocks = owners - 1
     padded = (blocks + 7) // 8 * 8
     spectra = jnp.pad(spectra, ((0, padded - blocks), (0, 0), (0, 0), (0, 0)))

time: 64.3 us -> 59.7 us (0.928)
  the two profiles are of different devices: /device:TPU:9 before, /device:TPU:3 now
where the time goes in v2:
time: 59.7 us; the launch traced here: 59.4 us
  Pallas kernels  41.2 us (69%)
  local copies, waits for them, and re-layouts  7.3 us (12%)
  blocking collectives  4.93 us (8%)
  matrix products  3.93 us (7%)
  other arithmetic  1.3 us (2%)
  between operations  0.76 us (1%)
    pallas_call x1, Pallas kernels, exchange(): pl.pallas_call(exchange_kernel, out_shape=jax.ShapeDtypeStruct((owners, r...  33.4 us
    pallas_call x1, Pallas kernels, subspace(): pl.pallas_call(functools.partial(subspace_kernel, modes), out_shape=(jax....  7.77 us
    psum x1, blocking collectives, body(): gram_re, gram_im = lax.psum((gram_re, gram_im), 'space')  4.93 us
    unnamed x12, local copies, waits for them, and re-layouts  4.69 us
    dot_general x1, matrix products, body(): grams = jnp.einsum('nrfc,msfc->frnsm', spectra, weighted, precision=precise)  3.38 us

profile of v2, /device:TPU:3, one launch (start us, length us, event | category | flops | bytes accessed | tf_op | source)
XLA Modules:
  0.0 59.4 jit_solution(16908539283321370302)
XLA Ops:
  0.6 0.0 copy-start
  0.6 1.4 %copy-done = f32[256,3,512]{2,0,1:T(8,128)S(1)} copy-done((f32[256,3,512]{2,0,1:T(8,128)S(1)}, f32[256,3,512]{2,0,1:T(8,128)}, u32[]{:S(2)}) %copy-start) | copy-done | bytes 1572888
  2.0 0.0 copy-start.1
  2.0 0.9 %copy-done.1 = f32[2,96,256]{2,1,0:T(8,128)S(1)} copy-done((f32[2,96,256]{2,1,0:T(8,128)S(1)}, f32[2,96,256]{2,1,0:T(8,128)}, u32[]{:S(2)}) %copy-start.1) | copy-done | bytes 196632
  3.0 33.4 %shard_map.59 = f32[16,24,768]{2,1,0:T(8,128)S(1)} custom-call(f32[2,96,256]{2,1,0:T(8,128)S(1)} %copy-done.1, f32[3,256,512]{2,1,0:T(8,128)S(1)} %bitcast.43), custom_call_target="tpu_custom_call" | custom-call | tf_op jit(solution)/shard_map/pallas_call | solution.py:110
  36.4 0.1 fusion.28
  36.5 0.4 copy.34
  36.9 0.4 copy.35
  37.3 0.2 copy_add_fusion
  37.6 0.1 fusion.1
  37.7 0.0 copy-start.4
  37.7 0.1 slice_bitcast_fusion.1
  37.7 0.6 %copy-done.4 = f32[512]{0:T(512)S(1)} copy-done((f32[512]{0:T(512)S(1)}, f32[512]{0:T(512)}, u32[]{:S(2)}) %copy-start.4) | copy-done | bytes 2072
  38.4 3.4 %fusion.4 = f32[4,16,2,16,2]{3,1,4,2,0:T(8,128)S(1)} fusion(f32[15,2,4,768]{3,0,1,2:T(8,128)S(1)} %get-tuple-element.19, f32[15,2,4,768]{3,0,1,2:T(8,128)S(1)} %get-tuple-element.18, f32[1536]{0:T(1024)S(1)} %mul.48), kind=kOutput, calls=%fused_computation.10 | convolution fusion | flops 77266944 | bytes 759808 | tf_op jit(solution)/shard_map/nrfc,msfc->frnsm/dot_general | solution.py:222
  41.8 0.0 copy-start.2
  41.8 0.5 copy.38
  42.3 4.9 %all-reduce.2 = (f32[16,16,4]{2,1,0:T(8,128)}, f32[16,16,4]{2,1,0:T(8,128)}) all-reduce(f32[16,16,4]{2,1,0:T(8,128)S(1)} %get-tuple-element.21, f32[16,16,4]{2,1,0:T(8,128)S(1)} %get-tuple-element.20), channel_id=1, replica_groups=mesh['tm'=16,'space'=2] {'space'}, use_global_device_ids=true, to_apply=%region_0.1 | all-reduce | flops 2048 | bytes 16384 | tf_op jit(solution)/shard_map/psum | solution.py:225
  47.2 0.0 copy-done.2
  47.2 0.8 %copy.39.start_ref = f32[2,8,16,1]{3,2,1,0:T(8,128)} copy(f32[2,8,16,1]{2,1,0,3:T(8,128)S(1)} %pad_bitcast_fusion) | data formatting | bytes 2048 | tf_op jit(solution)/shard_map/broadcast_in_dim | solution.py:190
  48.1 7.8 %shard_map.60 = (f32[2,8,16,4]{3,2,1,0:T(8,128)}, f32[8,4]{1,0:T(8,128)}) custom-call(f32[16,16,4]{2,1,0:T(8,128)} %get-tuple-element.14.mr_ref, f32[16,16,4]{2,1,0:T(8,128)} %get-tuple-element.15.mi_ref, f32[2,8,16,1]{3,2,1,0:T(8,128)} %copy.39.start_ref), custom_call_target="tpu_custom_call" | custom-call | tf_op jit(solution)/shard_map/pallas_call | solution.py:192
  55.8 0.9 %slice_negate_fusion = (f32[1,8,16,4]{3,2,1,0:T(8,128)S(1)}, f32[1,8,16,4]{3,2,1,0:T(8,128)S(1)}, f32[1,8,16,4]{3,2,1,0:T(8,128)S(1)}) fusion(f32[2,8,16,4]{3,2,1,0:T(8,128)} %get-tuple-element.4), kind=kLoop, calls=%fused_computation.45 | loop fusion | flops 512 | bytes 10240 | tf_op jit(solution)/shard_map/neg | solution.py:228
  56.7 0.1 copy.40
  56.8 0.1 copy.41
  56.9 0.1 copy.42
  57.1 0.0 copy-start.3
  57.1 0.6 fusion.2
  57.7 1.1 %copy.45 = f32[4,8,2,3,512]{4,2,3,1,0:T(2,128)} copy(f32[4,8,2,3,512]{4,1,3,2,0:T(8,128)S(1)} %bitcast.47) | data formatting | bytes 786432
  58.7 0.0 copy-done.3
  58.7 0.7 %copy.46 = f32[4,8]{1,0:T(4,128)} copy(f32[4,8]{0,1:T(8,128)S(1)} %bitcast.48) | data formatting | bytes 256
  (6 shorter events, 0.1 us)
Async XLA Ops:
  0.6 1.4 %copy-start = (f32[256,3,512]{2,0,1:T(8,128)S(1)}, f32[256,3,512]{2,0,1:T(8,128)}, u32[]{:S(2)}) copy-start(f32[256,3,512]{2,0,1:T(8,128)} %param.4) | copy-start | bytes 4718596
  2.0 0.9 %copy-start.1 = (f32[2,96,256]{2,1,0:T(8,128)S(1)}, f32[2,96,256]{2,1,0:T(8,128)}, u32[]{:S(2)}) copy-start(f32[2,96,256]{2,1,0:T(8,128)} %constant.45.clone.table_ref) | copy-start | bytes 589828
  37.7 0.7 %copy-start.4 = (f32[512]{0:T(512)S(1)}, f32[512]{0:T(512)}, u32[]{:S(2)}) copy-start(f32[512]{0:T(512)} %param.5) | copy-start | bytes 6148
  41.8 5.5 %copy-start.2 = (f32[2,15,8]{1,2,0:T(8,128)S(1)}, f32[2,15,8]{1,2,0:T(8,128)}, u32[]{:S(2)}) copy-start(f32[2,15,8]{1,2,0:T(8,128)} %param.6) | copy-start | bytes 2884
  57.1 1.6 %copy-start.3 = (f32[8,4]{1,0:T(8,128)S(1)}, f32[8,4]{1,0:T(8,128)}, u32[]{:S(2)}) copy-start(f32[8,4]{1,0:T(8,128)} %get-tuple-element.5) | copy-start | bytes 388

commit v3 on v2

--- a/solution.py
+++ b/solution.py
@@ -29,14 +29,19 @@
     return table.astype(np.float32)
 
 
-def exchange_kernel(table_ref, samples_ref, out_ref, send_ref, send_sems, recv_sems):
-    owners, rows, half = send_ref.shape
-    count = rows // 2
+def exchange_kernel(
+    table_ref, samples_ref, main_ref, edges_ref, main_out, edge_out, forward_out,
+    main_send, main_recv, edge_send, edge_recv, forward_send, forward_recv, last_send,
+):
+    owners, count, _ = main_ref.shape
+    freqs = count // 2
     points = samples_ref.shape[2]
+    quarter = edges_ref.shape[3]
     group = owners // 2
     me = lax.axis_index("tm")
     near = me // group
     far = 1 - near
+    last = owners - 1
 
     barrier = pltpu.get_barrier_semaphore()
 
@@ -45,7 +50,17 @@
         other = lax.rem(me + s, owners)
         pl.semaphore_signal(barrier, inc=1, device_id={"tm": other}, device_id_type=pl.DeviceIdType.MESH)
 
-    def transform(side):
+    def remote(source, target, sent, received, device):
+        return pltpu.make_async_remote_copy(
+            src_ref=source,
+            dst_ref=target,
+            send_sem=sent,
+            recv_sem=received,
+            device_id={"tm": device},
+            device_id_type=pl.DeviceIdType.MESH,
+        )
+
+    def transform(side, edged):
         for c in range(samples_ref.shape[0]):
             part = jnp.dot(
                 table_ref[side],
@@ -54,73 +69,186 @@
                 preferred_element_type=jnp.float32,
             )
             low, high = c * points, (c + 1) * points
-            for q in range(2):
-                begin, end = max(low, q * half), min(high, (q + 1) * half)
+            for i in range(group):
+                main_out[side * group + i, :, low:high] = part[i * count : (i + 1) * count]
+            for q in range(4):
+                begin, end = max(low, q * quarter), min(high, (q + 1) * quarter)
                 if begin >= end:
                     continue
-                for i in range(group):
-                    send_ref[
-                        side * group + i, q * count : (q + 1) * count, begin - q * half : end - q * half
-                    ] = part[i * count : (i + 1) * count, begin - low : end - low]
-
-    def copy(source, target):
-        return pltpu.make_async_remote_copy(
-            src_ref=send_ref.at[target],
-            dst_ref=out_ref.at[source],
-            send_sem=send_sems.at[target],
-            recv_sem=recv_sems.at[source],
-            device_id={"tm": target},
-            device_id_type=pl.DeviceIdType.MESH,
+                for i in edged:
+                    for edge in range(2):
+                        for r in range(2):
+                            row = group * count + i * 4 + edge * 2 + r
+                            edge_out[
+                                side * group + i,
+                                edge,
+                                r * 4 + q : r * 4 + q + 1,
+                                begin - q * quarter : end - q * quarter,
+                            ] = part[row : row + 1, begin - low : end - low]
+
+    def main_copy(slot, device):
+        return remote(main_out.at[device], main_ref.at[slot], main_send.at[device], main_recv.at[slot], device)
+
+    def edge_copy(slot, device):
+        return remote(edge_out.at[device], edges_ref.at[slot], edge_send.at[device], edge_recv.at[slot], device)
+
+    def last_copy():
+        return remote(
+            edge_out.at[last, 1], edges_ref.at[me, 1], last_send.at[0], forward_recv.at[me, 1], last
         )
 
-    transform(far)
+    def forward_copy(source, edge, device):
+        return remote(
+            forward_out.at[source, edge],
+            edges_ref.at[source, edge],
+            forward_send.at[source, edge],
+            forward_recv.at[source, edge],
+            device,
+        )
+
+    def pack(target, source, edge, freq, sign):
+        for r in range(2):
+            for q in range(4):
+                row = main_ref[source, r * freqs + freq : r * freqs + freq + 1, q * quarter : (q + 1) * quarter]
+                target[source, edge, r * 4 + q : r * 4 + q + 1, :] = row if r == 0 else sign * row
+
+    transform(far, [group - 1])
     pl.semaphore_wait(barrier, owners - 1)
 
     @pl.loop(0, group)
     def _(s):
-        copy(me, far * group + lax.rem(me + s, group)).start()
-
-    transform(near)
+        main_copy(me, far * group + lax.rem(me + s, group)).start()
+
+    @pl.when(near == 0)
+    def _():
+        last_copy().start()
+
+    transform(near, range(group))
 
     @pl.loop(1, group)
     def _(s):
-        copy(me, near * group + lax.rem(me + s, group)).start()
-
-    out_ref[me] = send_ref[me]
-
-    @pl.loop(1, owners)
-    def _(s):
-        other = lax.rem(me + s, owners)
-        copy(me, other).wait_send()
-        pltpu.make_async_remote_copy(
-            src_ref=send_ref.at[other],
-            dst_ref=out_ref.at[other],
-            send_sem=send_sems.at[other],
-            recv_sem=recv_sems.at[other],
-            device_id={"tm": other},
-            device_id_type=pl.DeviceIdType.MESH,
-        ).wait_recv()
+        other = near * group + lax.rem(me + s, group)
+        main_copy(me, other).start()
+        edge_copy(me, other).start()
+
+    main_ref[me] = main_out[me]
+    edges_ref[me] = edge_out[me]
+
+    lower = me - 1
+    upper = me + 1
+    inner_lower = jnp.logical_and(me > 0, lower // group == near)
+    inner_upper = jnp.logical_and(me < last, upper // group == near)
+    outer_lower = jnp.logical_and(me > 0, lower // group != near)
+    outer_upper = jnp.logical_and(me < last, upper // group != near)
+
+    def forward(source, to_lower, to_upper):
+        @pl.when(to_lower)
+        def _():
+            pack(forward_out, source, 1, 0, 1.0)
+            forward_copy(source, 1, lower).start()
+
+        @pl.when(to_upper)
+        def _():
+            pack(forward_out, source, 0, freqs - 1, 1.0)
+            forward_copy(source, 0, upper).start()
+
+    @pl.loop(0, group)
+    def _(s):
+        source = far * group + lax.rem(me - s + owners, group)
+        main_copy(source, source).wait_recv()
+        forward(source, inner_lower, inner_upper)
+
+    forward(me, outer_lower, outer_upper)
+
+    @pl.loop(1, group)
+    def _(s):
+        source = near * group + lax.rem(me - s + owners, group)
+        main_copy(source, source).wait_recv()
+        edge_copy(source, source).wait_recv()
+        forward(source, outer_lower, outer_upper)
+
+    @pl.loop(0, group)
+    def _(s):
+        source = far * group + s
+        main_copy(me, source).wait_send()
+        forward_copy(source, 1, lower).wait_recv()
+
+        @pl.when(me > 0)
+        def _():
+            forward_copy(source, 0, upper).wait_recv()
+
+        @pl.when(me == 0)
+        def _():
+            if freqs > 1:
+                pack(edges_ref, source, 0, 1, -1.0)
+            else:
+                edges_ref[source, 0, 0:4] = edges_ref[source, 1, 0:4]
+                edges_ref[source, 0, 4:8] = -edges_ref[source, 1, 4:8]
+
+        @pl.when(inner_lower)
+        def _():
+            forward_copy(source, 1, lower).wait_send()
+
+        @pl.when(inner_upper)
+        def _():
+            forward_copy(source, 0, upper).wait_send()
+
+    @pl.loop(0, group)
+    def _(s):
+        source = near * group + s
+
+        @pl.when(source != me)
+        def _():
+            main_copy(me, source).wait_send()
+            edge_copy(me, source).wait_send()
+
+        @pl.when(outer_lower)
+        def _():
+            forward_copy(source, 1, lower).wait_send()
+
+        @pl.when(outer_upper)
+        def _():
+            forward_copy(source, 0, upper).wait_send()
+
+    @pl.when(near == 0)
+    def _():
+        last_copy().wait_send()
 
 
 def exchange(table, samples):
     owners, parts, freqs, seg_len = table.shape
-    half = samples.shape[0] * samples.shape[2] // 2
-    rows = 2 * parts * freqs
+    group = owners // 2
+    columns = samples.shape[0] * samples.shape[2]
+    main = table[:, :, 1:-1].reshape(2, -1, seg_len)
+    edge = table[:, :, [0, freqs - 1]].swapaxes(1, 2).reshape(2, -1, seg_len)
+    rows = np.concatenate([main, edge], 1)
+    main_shape = (owners, parts * (freqs - 2), columns)
+    edge_shape = (owners, 2, 8, columns // 4)
     spec = pl.BlockSpec(memory_space=pltpu.VMEM)
     return pl.pallas_call(
         exchange_kernel,
-        out_shape=jax.ShapeDtypeStruct((owners, rows, half), jnp.float32),
+        out_shape=(
+            jax.ShapeDtypeStruct(main_shape, jnp.float32),
+            jax.ShapeDtypeStruct(edge_shape, jnp.float32),
+        ),
         in_specs=[spec] * 2,
-        out_specs=spec,
+        out_specs=(spec, spec),
         scratch_shapes=[
-            pltpu.VMEM((owners, rows, half), jnp.float32),
+            pltpu.VMEM(main_shape, jnp.float32),
+            pltpu.VMEM(edge_shape, jnp.float32),
+            pltpu.VMEM(edge_shape, jnp.float32),
             pltpu.SemaphoreType.DMA((owners,)),
             pltpu.SemaphoreType.DMA((owners,)),
+            pltpu.SemaphoreType.DMA((owners,)),
+            pltpu.SemaphoreType.DMA((owners,)),
+            pltpu.SemaphoreType.DMA((owners, 2)),
+            pltpu.SemaphoreType.DMA((owners, 2)),
+            pltpu.SemaphoreType.DMA((1,)),
         ],
         compiler_params=pltpu.CompilerParams(
             collective_id=0, has_side_effects=True, vmem_limit_bytes=40 * 1024 * 1024
         ),
-    )(table.reshape(2, -1, seg_len), samples)
+    )(rows, samples)
 
 
 def subspace_kernel(modes, mr_ref, mi_ref, start_ref, vec_ref, energy_ref):
@@ -207,12 +335,14 @@
     owners = lax.axis_size("tm")
     freqs = NF // owners
     table = segment_table(owners, seg_len)
-    arrived = exchange(table, samples).reshape(owners, 2, 2, freqs + 2, columns // 2)
+    main, edges = exchange(table, samples)
+    main = main.reshape(owners, 2, freqs, columns)
+    edges = edges.reshape(owners, 2, 2, 1, columns)
+    arrived = jnp.concatenate([edges[:, 0], main, edges[:, 1]], 2)
     first = lax.axis_index("tm") * freqs - 1
     signs = 1.0 - 2.0 * jnp.mod(first + owners * freqs * 2 + jnp.arange(freqs + 2), 2).astype(jnp.float32)
     pairs = arrived[:-1] + signs[:, None] * arrived[1:]
     spectra = 0.5 * pairs[..., 1:-1, :] - 0.25 * (pairs[..., :-2, :] + pairs[..., 2:, :])
-    spectra = jnp.concatenate([spectra[:, 0], spectra[:, 1]], -1)
     blocks = owners - 1
     padded = (blocks + 7) // 8 * 8
     spectra = jnp.pad(spectra, ((0, padded - blocks), (0, 0), (0, 0), (0, 0)))

time: 59.7 us -> 56.5 us (0.946)
  the two profiles are of different devices: /device:TPU:3 before, /device:TPU:17 now
where the time goes in v3:
time: 56.5 us; the launch traced here: 56.2 us
  Pallas kernels  36.7 us (65%)
  local copies, waits for them, and re-layouts  7.27 us (13%)
  blocking collectives  6.22 us (11%)
  matrix products  3.9 us (7%)
  other arithmetic  1.38 us (2%)
  between operations  0.76 us (1%)
    pallas_call x1, Pallas kernels, exchange(): pl.pallas_call(exchange_kernel, out_shape=(jax.ShapeDtypeStruct(main_shap...  28.9 us
    pallas_call x1, Pallas kernels, subspace(): pl.pallas_call(functools.partial(subspace_kernel, modes), out_shape=(jax....  7.79 us
    psum x1, blocking collectives, body(): gram_re, gram_im = lax.psum((gram_re, gram_im), 'space')  6.22 us
    unnamed x12, local copies, waits for them, and re-layouts  4.61 us
    dot_general x1, matrix products, body(): grams = jnp.einsum('nrfc,msfc->frnsm', spectra, weighted, precision=precise)  3.37 us

profile of v3, /device:TPU:17, one launch (start us, length us, event | category | flops | bytes accessed | tf_op | source)
XLA Modules:
  0.0 56.2 jit_solution(4494006162616217904)
XLA Ops:
  0.6 0.0 copy-start
  0.6 1.4 %copy-done = f32[256,3,512]{2,0,1:T(8,128)S(1)} copy-done((f32[256,3,512]{2,0,1:T(8,128)S(1)}, f32[256,3,512]{2,0,1:T(8,128)}, u32[]{:S(2)}) %copy-start) | copy-done | bytes 1572888
  2.0 0.0 copy-start.1
  2.0 0.9 %copy-done.1 = f32[2,96,256]{2,1,0:T(8,128)S(1)} copy-done((f32[2,96,256]{2,1,0:T(8,128)S(1)}, f32[2,96,256]{2,1,0:T(8,128)}, u32[]{:S(2)}) %copy-start.1) | copy-done | bytes 196632
  3.0 28.9 %shard_map.59 = (f32[16,8,1536]{2,1,0:T(8,128)S(1)}, f32[16,2,8,384]{3,2,1,0:T(8,128)S(1)}) custom-call(f32[2,96,256]{2,1,0:T(8,128)S(1)} %copy-done.1, f32[3,256,512]{2,1,0:T(8,128)S(1)} %bitcast.43), custom_call_target="tpu_custom_call" | custom-call | tf_op jit(solution)/shard_map/pallas_call | solution.py:228
  31.9 0.2 reshape.39
  32.1 0.1 copy_bitcast_fusion
  32.2 0.2 reshape.40
  32.5 0.5 copy.35
  32.9 0.1 pad_maximum_fusion
  33.0 0.2 fusion
  33.3 0.0 copy-start.4
  33.3 0.1 fusion.2
  33.4 0.5 copy-done.4
  34.0 3.4 %fusion.5 = f32[4,16,2,16,2]{3,1,4,2,0:T(8,128)S(1)} fusion(f32[15,2,4,1536]{3,0,1,2:T(8,128)S(1)} %fusion.2, f32[1536]{0:T(1024)S(1)} %mul.48), kind=kOutput, calls=%fused_computation.9 | convolution fusion | flops 75694080 | bytes 759808 | tf_op jit(solution)/shard_map/nrfc,msfc->frnsm/dot_general | solution.py:352
  37.3 0.0 copy-start.2
  37.4 0.5 copy.36
  37.9 6.2 %all-reduce.2 = (f32[16,16,4]{2,1,0:T(8,128)}, f32[16,16,4]{2,1,0:T(8,128)}) all-reduce(f32[16,16,4]{2,1,0:T(8,128)S(1)} %get-tuple-element.21, f32[16,16,4]{2,1,0:T(8,128)S(1)} %get-tuple-element.20), channel_id=1, replica_groups=mesh['tm'=16,'space'=2] {'space'}, use_global_device_ids=true, to_apply=%region_0.1 | all-reduce | flops 2048 | bytes 16384 | tf_op jit(solution)/shard_map/psum | solution.py:355
  44.1 0.0 copy-done.2
  44.1 0.8 %copy.37.start_ref = f32[2,8,16,1]{3,2,1,0:T(8,128)} copy(f32[2,8,16,1]{2,1,0,3:T(8,128)S(1)} %pad_bitcast_fusion) | data formatting | bytes 2048 | tf_op jit(solution)/shard_map/broadcast_in_dim | solution.py:318
  44.9 7.8 %shard_map.60 = (f32[2,8,16,4]{3,2,1,0:T(8,128)}, f32[8,4]{1,0:T(8,128)}) custom-call(f32[16,16,4]{2,1,0:T(8,128)} %get-tuple-element.18.mr_ref, f32[16,16,4]{2,1,0:T(8,128)} %get-tuple-element.19.mi_ref, f32[2,8,16,1]{3,2,1,0:T(8,128)} %copy.37.start_ref), custom_call_target="tpu_custom_call" | custom-call | tf_op jit(solution)/shard_map/pallas_call | solution.py:320
  52.7 0.9 %slice_negate_fusion = (f32[1,8,16,4]{3,2,1,0:T(8,128)S(1)}, f32[1,8,16,4]{3,2,1,0:T(8,128)S(1)}, f32[1,8,16,4]{3,2,1,0:T(8,128)S(1)}) fusion(f32[2,8,16,4]{3,2,1,0:T(8,128)} %get-tuple-element.8), kind=kLoop, calls=%fused_computation.38 | loop fusion | flops 512 | bytes 10240 | tf_op jit(solution)/shard_map/neg | solution.py:358
  53.6 0.1 copy.38
  53.7 0.0 copy-start.3
  53.7 0.1 copy.39
  53.9 0.1 copy.40
  54.0 0.5 fusion.3
  54.5 1.1 %copy.43 = f32[4,8,2,3,512]{4,2,3,1,0:T(2,128)} copy(f32[4,8,2,3,512]{4,1,3,2,0:T(8,128)S(1)} %bitcast.45) | data formatting | bytes 786432
  55.6 0.0 copy-done.3
  55.6 0.7 %copy.44 = f32[4,8]{1,0:T(4,128)} copy(f32[4,8]{0,1:T(8,128)S(1)} %bitcast.46) | data formatting | bytes 256
  (7 shorter events, 0.1 us)
Async XLA Ops:
  0.6 1.4 %copy-start = (f32[256,3,512]{2,0,1:T(8,128)S(1)}, f32[256,3,512]{2,0,1:T(8,128)}, u32[]{:S(2)}) copy-start(f32[256,3,512]{2,0,1:T(8,128)} %param.4) | copy-start | bytes 4718596
  2.0 0.9 %copy-start.1 = (f32[2,96,256]{2,1,0:T(8,128)S(1)}, f32[2,96,256]{2,1,0:T(8,128)}, u32[]{:S(2)}) copy-start(f32[2,96,256]{2,1,0:T(8,128)} %constant.45.clone.table_ref) | copy-start | bytes 589828
  33.3 0.7 %copy-start.4 = (f32[512]{0:T(512)S(1)}, f32[512]{0:T(512)}, u32[]{:S(2)}) copy-start(f32[512]{0:T(512)} %param.5) | copy-start | bytes 6148
  37.3 6.8 %copy-start.2 = (f32[2,15,8]{1,2,0:T(8,128)S(1)}, f32[2,15,8]{1,2,0:T(8,128)}, u32[]{:S(2)}) copy-start(f32[2,15,8]{1,2,0:T(8,128)} %param.6) | copy-start | bytes 2884
  53.7 1.9 %copy-start.3 = (f32[8,4]{1,0:T(8,128)S(1)}, f32[8,4]{1,0:T(8,128)}, u32[]{:S(2)}) copy-start(f32[8,4]{1,0:T(8,128)} %get-tuple-element.9) | copy-start | bytes 388

commit v4 on v3

--- a/solution.py
+++ b/solution.py
@@ -251,8 +251,63 @@
     )(rows, samples)
 
 
-def subspace_kernel(modes, mr_ref, mi_ref, start_ref, vec_ref, energy_ref):
-    n = mr_ref.shape[0]
+def modes_kernel(
+    modes, total_points, spectra_ref, weights_ref, start_ref, out_ref, energy_ref,
+    gram_ref, mine_ref, mr_ref, mi_ref, send_sems, recv_sems,
+):
+    freqs, double, columns = spectra_ref.shape
+    n = double // 2
+    lanes = freqs * double
+    devices = gram_ref.shape[0]
+    me = lax.axis_index("space")
+
+    barrier = pltpu.get_barrier_semaphore()
+    for s in range(1, devices):
+        other = lax.rem(me + s, devices)
+        pl.semaphore_signal(barrier, inc=1, device_id={"space": other}, device_id_type=pl.DeviceIdType.MESH)
+
+    rows = spectra_ref[...].reshape(lanes, columns)
+    grams = lax.dot_general(
+        rows,
+        rows * weights_ref[...],
+        (((1,), (1,)), ((), ())),
+        precision=precise,
+        preferred_element_type=jnp.float32,
+    )
+    owner = lax.broadcasted_iota(jnp.int32, (n, lanes), 1) // double
+    top = grams[:n]
+    low = grams[n:double]
+    for f in range(1, freqs):
+        top = jnp.where(owner == f, grams[f * double : f * double + n], top)
+        low = jnp.where(owner == f, grams[f * double + n : (f + 1) * double], low)
+    mine_ref[0] = (top + pltpu.roll(low, lanes - n, 1)) / total_points
+    mine_ref[1] = (pltpu.roll(top, lanes - n, 1) - low) / total_points
+
+    def copy(slot, device):
+        return pltpu.make_async_remote_copy(
+            src_ref=mine_ref,
+            dst_ref=gram_ref.at[slot],
+            send_sem=send_sems.at[device],
+            recv_sem=recv_sems.at[slot],
+            device_id={"space": device},
+            device_id_type=pl.DeviceIdType.MESH,
+        )
+
+    pl.semaphore_wait(barrier, devices - 1)
+    for s in range(1, devices):
+        copy(me, lax.rem(me + s, devices)).start()
+    gram_ref[me] = mine_ref[...]
+    for s in range(1, devices):
+        other = lax.rem(me + s, devices)
+        copy(other, other).wait_recv()
+    gram_re = gram_ref[0, 0]
+    gram_im = gram_ref[0, 1]
+    for d in range(1, devices):
+        gram_re = gram_re + gram_ref[d, 0]
+        gram_im = gram_im + gram_ref[d, 1]
+    for j in range(n):
+        mr_ref[j] = pltpu.roll(gram_re, lanes - j, 1) if j else gram_re
+        mi_ref[j] = pltpu.roll(gram_im, lanes - j, 1) if j else gram_im
 
     def apply(vec):
         out = []
@@ -302,30 +357,64 @@
     flat = lax.fori_loop(0, ITERS, sweep, flat)
     vec = [(flat[2 * k], flat[2 * k + 1]) for k in range(modes)]
     images = apply(vec)
+    place = lax.rem(lax.broadcasted_iota(jnp.int32, (n, lanes), 1), double)
+    mix_re = mix_im = jnp.zeros((n, lanes), jnp.float32)
     for k in range(modes):
         (vr, vi), (wr, wi) = vec[k], images[k]
         energy = total(vr * wr + vi * wi)
         inverse = 1.0 / jnp.sqrt(energy + epsilon)
         energy_ref[k : k + 1] = energy
-        vec_ref[0, k] = vr * inverse
-        vec_ref[1, k] = vi * inverse
-
-
-def subspace(gram_re, gram_im, start):
-    freqs, n, _ = gram_re.shape
+        vr, vi = vr * inverse, vi * inverse
+        for part, (real, imag) in enumerate(((vr, -vi), (vi, vr))):
+            slot = 2 * k + part
+            if slot:
+                real, imag = pltpu.roll(real, slot, 1), pltpu.roll(imag, slot, 1)
+            mix_re = jnp.where(place == slot, real, mix_re)
+            mix_im = jnp.where(place == slot, imag, mix_im)
+    mix = jnp.concatenate([mix_re, mix_im], 0).T
+    width = out_ref.shape[3]
+    for f in range(freqs):
+        result = jnp.dot(
+            mix[f * double : f * double + 2 * modes],
+            spectra_ref[f],
+            precision=precise,
+            preferred_element_type=jnp.float32,
+        )
+        for c in range(columns // width):
+            out_ref[c, f] = result[:, c * width : (c + 1) * width]
+    for s in range(1, devices):
+        copy(me, lax.rem(me + s, devices)).wait_send()
+
+
+def find_modes(spectra, col_weights, start, total_points, components):
+    freqs, double, columns = spectra.shape
+    n = double // 2
+    lanes = freqs * double
     modes = start.shape[2]
+    devices = lax.axis_size("space")
     start = jnp.pad(start, ((0, 0), (0, n - start.shape[1]), (0, 0)))
     start = start.transpose(0, 2, 1)[..., None]
     spec = pl.BlockSpec(memory_space=pltpu.VMEM)
     return pl.pallas_call(
-        functools.partial(subspace_kernel, modes),
+        functools.partial(modes_kernel, modes, total_points),
         out_shape=(
-            jax.ShapeDtypeStruct((2, modes, n, freqs), jnp.float32),
-            jax.ShapeDtypeStruct((modes, freqs), jnp.float32),
+            jax.ShapeDtypeStruct((components, freqs, 2 * modes, columns // components), jnp.float32),
+            jax.ShapeDtypeStruct((modes, lanes), jnp.float32),
         ),
         in_specs=[spec] * 3,
         out_specs=(spec, spec),
-    )(gram_re.transpose(2, 1, 0), gram_im.transpose(2, 1, 0), start)
+        scratch_shapes=[
+            pltpu.VMEM((devices, 2, n, lanes), jnp.float32),
+            pltpu.VMEM((2, n, lanes), jnp.float32),
+            pltpu.VMEM((n, n, lanes), jnp.float32),
+            pltpu.VMEM((n, n, lanes), jnp.float32),
+            pltpu.SemaphoreType.DMA((devices,)),
+            pltpu.SemaphoreType.DMA((devices,)),
+        ],
+        compiler_params=pltpu.CompilerParams(
+            collective_id=1, has_side_effects=True, vmem_limit_bytes=40 * 1024 * 1024
+        ),
+    )(spectra, col_weights, start)
 
 
 def body(snapshots, weights, start):
@@ -346,18 +435,12 @@
     blocks = owners - 1
     padded = (blocks + 7) // 8 * 8
     spectra = jnp.pad(spectra, ((0, padded - blocks), (0, 0), (0, 0), (0, 0)))
-    col_weights = jnp.tile(weights, components)
+    col_weights = jnp.tile(weights, components)[None]
     total_points = points * lax.axis_size("space")
-    weighted = spectra * col_weights
-    grams = jnp.einsum("nrfc,msfc->frnsm", spectra, weighted, precision=precise)
-    gram_re = (grams[:, 0, :, 0, :] + grams[:, 1, :, 1, :]) / total_points
-    gram_im = (grams[:, 0, :, 1, :] - grams[:, 1, :, 0, :]) / total_points
-    gram_re, gram_im = lax.psum((gram_re, gram_im), "space")
-    vec, energy = subspace(gram_re, gram_im, start)
-    vr, vi = vec[0], vec[1]
-    mix = jnp.stack([jnp.stack([vr, -vi], 0), jnp.stack([vi, vr], 0)], 0)
-    modes = jnp.einsum("nrfc,srknf->fksc", spectra, mix, precision=precise)
-    return modes.reshape(freqs, modes.shape[1], 2, components, points), energy.T
+    spectra = spectra.transpose(2, 1, 0, 3).reshape(freqs, 2 * padded, columns)
+    modes, energy = find_modes(spectra, col_weights, start, total_points, components)
+    modes = modes.reshape(components, freqs, start.shape[2], 2, points).transpose(1, 2, 3, 0, 4)
+    return modes, energy[:, :: 2 * padded].T
 
 
 def solution(mesh):

time: 56.5 us -> 47.3 us (0.84)
  blocking collectives: 6.22 us -> 0 us
  matrix products: 3.9 us -> 0 us
  Pallas kernels: 36.7 us -> 40 us
  local copies, waits for them, and re-layouts: 7.27 us -> 5.94 us
  other arithmetic: 1.38 us -> 0.46 us
    psum x1 -> x0, blocking collectives: 6.22 us -> none  [body(): gram_re, gram_im = lax.psum((gram_re, gram_im), 'space')]
    dot_general x2 -> x0, matrix products: 3.9 us -> none  [the longest x1 3.37 us: body(): grams = jnp.einsum('nrfc,msfc->frnsm', spectra, weighted, precision=precise)]
    pallas_call x1, Pallas kernels: 7.79 us -> 11 us  [find_modes(): pl.pallas_call(functools.partial(modes_kernel, modes, total_points), out_...]
    reshape x0 -> x2, local copies, waits for them, and re-layouts: none -> 1 us  [body(): modes.reshape(components, freqs, start.shape[2], 2, points)]
    unnamed x12 -> x11, local copies, waits for them, and re-layouts: 4.61 us -> 3.64 us
    neg x1 -> x0, other arithmetic: 0.88 us -> none  [body(): mix = jnp.stack([jnp.stack([vr, -vi], 0), jnp.stack([vi, vr], 0)], 0)]
    broadcast_in_dim x2, local copies, waits for them, and re-layouts: 0.85 us -> 0.18 us  [find_modes(): start = start.transpose(0, 2, 1)[..., None]]
where the time goes in v4:
time: 47.3 us; the launch traced here: 47.1 us
  Pallas kernels  40 us (85%)
  local copies, waits for them, and re-layouts  5.94 us (13%)
  between operations  0.76 us (2%)
    pallas_call x1, Pallas kernels, exchange(): pl.pallas_call(exchange_kernel, out_shape=(jax.ShapeDtypeStruct(main_shap...  28.9 us
    pallas_call x1, Pallas kernels, find_modes(): pl.pallas_call(functools.partial(modes_kernel, modes, total_points), out_...  11 us
    unnamed x11, local copies, waits for them, and re-layouts  3.64 us
    reshape x2, local copies, waits for them, and re-layouts, body(): modes.reshape(components, freqs, start.shape[2], 2, points)  1 us

profile of v4, /device:TPU:17, one launch (start us, length us, event | category | flops | bytes accessed | tf_op | source)
XLA Modules:
  0.0 47.1 jit_solution(8673493663927152090)
XLA Ops:
  0.6 0.0 copy-start
  0.6 0.0 copy-start.1
  0.7 1.4 %copy-done.1 = f32[256,3,512]{2,0,1:T(8,128)S(1)} copy-done((f32[256,3,512]{2,0,1:T(8,128)S(1)}, f32[256,3,512]{2,0,1:T(8,128)}, u32[]{:S(2)}) %copy-start.1) | copy-done | bytes 1572888
  2.1 0.0 copy-start.2
  2.1 0.9 %copy-done.2 = f32[2,96,256]{2,1,0:T(8,128)S(1)} copy-done((f32[2,96,256]{2,1,0:T(8,128)S(1)}, f32[2,96,256]{2,1,0:T(8,128)}, u32[]{:S(2)}) %copy-start.2) | copy-done | bytes 196632
  3.0 28.9 %shard_map.59 = (f32[16,8,1536]{2,1,0:T(8,128)S(1)}, f32[16,2,8,384]{3,2,1,0:T(8,128)S(1)}) custom-call(f32[2,96,256]{2,1,0:T(8,128)S(1)} %copy-done.2, f32[3,256,512]{2,1,0:T(8,128)S(1)} %bitcast.25), custom_call_target="tpu_custom_call" | custom-call | tf_op jit(solution)/shard_map/pallas_call | solution.py:228
  31.9 0.2 reshape.35
  32.2 0.1 copy_bitcast_fusion.1
  32.3 0.2 reshape.36
  32.5 0.5 copy.13
  33.0 0.1 pad_maximum_fusion
  33.1 0.2 fusion
  33.3 0.1 fusion.2
  33.4 0.0 copy-start.3
  33.5 0.1 pad.8
  33.5 0.6 %copy-done.3 = f32[2,15,8]{1,2,0:T(8,128)S(1)} copy-done((f32[2,15,8]{1,2,0:T(8,128)S(1)}, f32[2,15,8]{1,2,0:T(8,128)}, u32[]{:S(2)}) %copy-start.3) | copy-done | bytes 984
  34.1 0.2 copy.14.start_ref
  34.3 0.0 copy-done
  34.3 11.0 %shard_map.60 = (f32[3,4,16,512]{3,2,1,0:T(8,128)S(1)}, f32[8,128]{1,0:T(8,128)S(1)}) custom-call(f32[4,32,1536]{2,1,0:T(8,128)S(1)} %bitcast.24, f32[1,1536]{1,0:T(1,128)S(1)} %bitcast.26, f32[2,8,16,1]{3,2,1,0:T(8,128)S(1)} %copy.14.start_ref), custom_call_target="tpu_custom_call" | custom-call | tf_op jit(solution)/shard_map/pallas_call | solution.py:398
  45.4 0.2 reshape.38
  45.6 0.8 %copy.23 = f32[3,4,8,2,512]{4,3,0,2,1:T(2,128)} copy(f32[3,4,8,2,512]{4,3,2,1,0:T(2,128)S(1)} %reshape.38) | data formatting | bytes 786432 | tf_op jit(solution)/shard_map/reshape | solution.py:442
  46.4 0.1 slice.31
  46.5 0.7 %copy.16 = f32[4,8]{1,0:T(4,128)} copy(f32[4,8]{0,1:T(8,128)S(1)} %bitcast.28) | data formatting | bytes 256
  (5 shorter events, 0.1 us)
Async XLA Ops:
  0.6 33.7 %copy-start = (f32[512]{0:T(512)S(1)}, f32[512]{0:T(512)}, u32[]{:S(2)}) copy-start(f32[512]{0:T(512)} %param.5) | copy-start | bytes 6148
  0.6 1.4 %copy-start.1 = (f32[256,3,512]{2,0,1:T(8,128)S(1)}, f32[256,3,512]{2,0,1:T(8,128)}, u32[]{:S(2)}) copy-start(f32[256,3,512]{2,0,1:T(8,128)} %param.4) | copy-start | bytes 4718596
  2.1 0.9 %copy-start.2 = (f32[2,96,256]{2,1,0:T(8,128)S(1)}, f32[2,96,256]{2,1,0:T(8,128)}, u32[]{:S(2)}) copy-start(f32[2,96,256]{2,1,0:T(8,128)} %constant.41.clone.table_ref) | copy-start | bytes 589828
  33.4 0.7 %copy-start.3 = (f32[2,15,8]{1,2,0:T(8,128)S(1)}, f32[2,15,8]{1,2,0:T(8,128)}, u32[]{:S(2)}) copy-start(f32[2,15,8]{1,2,0:T(8,128)} %param.6) | copy-start | bytes 2884

commit v5 on v4

--- a/solution.py
+++ b/solution.py
@@ -372,7 +372,7 @@
             mix_re = jnp.where(place == slot, real, mix_re)
             mix_im = jnp.where(place == slot, imag, mix_im)
     mix = jnp.concatenate([mix_re, mix_im], 0).T
-    width = out_ref.shape[3]
+    width = out_ref.shape[4]
     for f in range(freqs):
         result = jnp.dot(
             mix[f * double : f * double + 2 * modes],
@@ -381,7 +381,8 @@
             preferred_element_type=jnp.float32,
         )
         for c in range(columns // width):
-            out_ref[c, f] = result[:, c * width : (c + 1) * width]
+            for k in range(modes):
+                out_ref[f, k, c] = result[2 * k : 2 * k + 2, c * width : (c + 1) * width]
     for s in range(1, devices):
         copy(me, lax.rem(me + s, devices)).wait_send()
 
@@ -398,7 +399,7 @@
     return pl.pallas_call(
         functools.partial(modes_kernel, modes, total_points),
         out_shape=(
-            jax.ShapeDtypeStruct((components, freqs, 2 * modes, columns // components), jnp.float32),
+            jax.ShapeDtypeStruct((freqs, modes, components, 2, columns // components), jnp.float32),
             jax.ShapeDtypeStruct((modes, lanes), jnp.float32),
         ),
         in_specs=[spec] * 3,
@@ -439,7 +440,7 @@
     total_points = points * lax.axis_size("space")
     spectra = spectra.transpose(2, 1, 0, 3).reshape(freqs, 2 * padded, columns)
     modes, energy = find_modes(spectra, col_weights, start, total_points, components)
-    modes = modes.reshape(components, freqs, start.shape[2], 2, points).transpose(1, 2, 3, 0, 4)
+    modes = modes.swapaxes(2, 3)
     return modes, energy[:, :: 2 * padded].T
 
 

time: 47.3 us -> 47.1 us (level)
    reshape x2 -> x0, local copies, waits for them, and re-layouts: 1 us -> none  [body(): modes.reshape(components, freqs, start.shape[2], 2, points)]
    unnamed x11 -> x12, local copies, waits for them, and re-layouts: 3.64 us -> 4.38 us
where the time goes in v5:
time: 47.1 us; the launch traced here: 46.9 us
  Pallas kernels  40 us (85%)
  local copies, waits for them, and re-layouts  5.69 us (12%)
  between operations  0.76 us (2%)
    pallas_call x1, Pallas kernels, exchange(): pl.pallas_call(exchange_kernel, out_shape=(jax.ShapeDtypeStruct(main_shap...  28.9 us
    pallas_call x1, Pallas kernels, find_modes(): pl.pallas_call(functools.partial(modes_kernel, modes, total_points), out_...  11 us
    unnamed x12, local copies, waits for them, and re-layouts  4.38 us

profile of v5, /device:TPU:17, one launch (start us, length us, event | category | flops | bytes accessed | tf_op | source)
XLA Modules:
  0.0 46.9 jit_solution(1113064028942163699)
XLA Ops:
  0.6 0.0 copy-start
  0.6 0.0 copy-start.1
  0.7 1.4 %copy-done.1 = f32[256,3,512]{2,0,1:T(8,128)S(1)} copy-done((f32[256,3,512]{2,0,1:T(8,128)S(1)}, f32[256,3,512]{2,0,1:T(8,128)}, u32[]{:S(2)}) %copy-start.1) | copy-done | bytes 1572888
  2.1 0.0 copy-start.2
  2.1 0.9 %copy-done.2 = f32[2,96,256]{2,1,0:T(8,128)S(1)} copy-done((f32[2,96,256]{2,1,0:T(8,128)S(1)}, f32[2,96,256]{2,1,0:T(8,128)}, u32[]{:S(2)}) %copy-start.2) | copy-done | bytes 196632
  3.0 28.9 %shard_map.59 = (f32[16,8,1536]{2,1,0:T(8,128)S(1)}, f32[16,2,8,384]{3,2,1,0:T(8,128)S(1)}) custom-call(f32[2,96,256]{2,1,0:T(8,128)S(1)} %copy-done.2, f32[3,256,512]{2,1,0:T(8,128)S(1)} %bitcast.21), custom_call_target="tpu_custom_call" | custom-call | tf_op jit(solution)/shard_map/pallas_call | solution.py:228
  31.9 0.2 reshape.32
  32.2 0.1 copy_bitcast_fusion
  32.3 0.2 reshape.33
  32.5 0.5 copy.12
  33.0 0.1 pad_maximum_fusion
  33.1 0.2 fusion
  33.3 0.1 fusion.2
  33.4 0.0 copy-start.3
  33.5 0.1 pad.8
  33.5 0.6 %copy-done.3 = f32[2,15,8]{1,2,0:T(8,128)S(1)} copy-done((f32[2,15,8]{1,2,0:T(8,128)S(1)}, f32[2,15,8]{1,2,0:T(8,128)}, u32[]{:S(2)}) %copy-start.3) | copy-done | bytes 984
  34.1 0.2 copy.13.start_ref
  34.3 0.0 copy-done
  34.3 11.0 %shard_map.60 = (f32[4,8,3,2,512]{4,3,2,1,0:T(2,128)S(1)}, f32[8,128]{1,0:T(8,128)S(1)}) custom-call(f32[4,32,1536]{2,1,0:T(8,128)S(1)} %bitcast.20, f32[1,1536]{1,0:T(1,128)S(1)} %bitcast.23, f32[2,8,16,1]{3,2,1,0:T(8,128)S(1)} %copy.13.start_ref), custom_call_target="tpu_custom_call" | custom-call | tf_op jit(solution)/shard_map/pallas_call | solution.py:399
  45.4 0.1 slice.31
  45.5 0.7 %copy.14 = f32[4,8]{1,0:T(4,128)} copy(f32[4,8]{0,1:T(8,128)S(1)} %bitcast.24) | data formatting | bytes 256
  46.1 0.7 %copy.21 = f32[4,8,2,3,512]{4,2,3,1,0:T(2,128)} copy(f32[4,8,2,3,512]{4,2,3,1,0:T(2,128)S(1)} %bitcast.22) | data formatting | bytes 786432
  (5 shorter events, 0.1 us)
Async XLA Ops:
  0.6 33.7 %copy-start = (f32[512]{0:T(512)S(1)}, f32[512]{0:T(512)}, u32[]{:S(2)}) copy-start(f32[512]{0:T(512)} %param.5) | copy-start | bytes 6148
  0.6 1.4 %copy-start.1 = (f32[256,3,512]{2,0,1:T(8,128)S(1)}, f32[256,3,512]{2,0,1:T(8,128)}, u32[]{:S(2)}) copy-start(f32[256,3,512]{2,0,1:T(8,128)} %param.4) | copy-start | bytes 4718596
  2.1 0.9 %copy-start.2 = (f32[2,96,256]{2,1,0:T(8,128)S(1)}, f32[2,96,256]{2,1,0:T(8,128)}, u32[]{:S(2)}) copy-start(f32[2,96,256]{2,1,0:T(8,128)} %constant.41.clone.table_ref) | copy-start | bytes 589828
  33.4 0.7 %copy-start.3 = (f32[2,15,8]{1,2,0:T(8,128)S(1)}, f32[2,15,8]{1,2,0:T(8,128)}, u32[]{:S(2)}) copy-start(f32[2,15,8]{1,2,0:T(8,128)} %param.6) | copy-start | bytes 2884
